TPU v7x, 256 devices: a whole 4x4x8 slice. The times are simulated.
256 devices in a mesh: batch: 16 (over z, core), proto: 16 (over y, x).
Axes of the slice: x: 4, y: 4, z: 8, core: 2. Of those that a mesh axis runs over, the one named last changes fastest.
Arguments:
- student_features: bfloat16 [10, 2048, 256], P(None, 'batch'), may hold values from -8 to 8
- teacher_features: bfloat16 [2, 2048, 256], P(None, 'batch'), may hold values from -8 to 8
- student_prototypes: bfloat16 [256, 65536], P(None, 'proto'), may hold values from -0.5 to 0.5
- teacher_prototypes: bfloat16 [256, 65536], P(None, 'proto'), may hold values from -0.5 to 0.5
Outputs:
- mean_loss: float32 [], replicated
- grad_features: float32 [10, 2048, 256], P(None, ('batch', 'proto'))
- grad_prototypes: float32 [256, 65536], P('batch', 'proto')
All inputs are finite; a program needn't handle non-finite values.
Results may differ from a plain program's by a relative error of at most 0.001.
The roundings to bfloat16 on the way count: a program that leaves them out, or rounds other values in their place, can miss the bound.
Values sent between devices are 32-bit elements; how exact they have to be, the bound alone decides.
A program may use at most 192 MiB of HBM per device.

v0:
```python
import jax
import jax.numpy as jnp
from jax import lax
from jax.sharding import PartitionSpec as P

CLUSTER_NUMBER = 65536
WIDE_CROP_NUMBER = 2
SK_ITERS = 3
PAIRS = 18
STUDENT_TEMP = 0.1
TEACHER_TEMP = 0.07
NORM_EPS = 1e-06


def unit_rows(values):
    floats = values.astype(jnp.float32)
    inverse = lax.rsqrt(jnp.sum(floats * floats, axis=-1, keepdims=True) + NORM_EPS)
    return (floats * inverse, inverse)


def unit_columns(values):
    floats = values.astype(jnp.float32)
    inverse = lax.rsqrt(jnp.sum(floats * floats, axis=0, keepdims=True) + NORM_EPS)
    return (floats * inverse, inverse)


def proto_step(cluster_share):
    column_mass = lax.psum(jnp.sum(cluster_share, axis=0), "batch")
    return cluster_share / (CLUSTER_NUMBER * column_mass[None, :])


def full_sweep(cluster_share, sample_number):
    cluster_share = proto_step(cluster_share)
    row_mass = lax.psum(jnp.sum(cluster_share, axis=1), "proto")
    return cluster_share / (sample_number * row_mass[:, None])


def on_device(student_features, teacher_features, student_prototypes, teacher_prototypes):
    crop_count, img_local, feature_dim = student_features.shape
    proto_local = student_prototypes.shape[1]
    batch_devices = lax.axis_size("batch")
    proto_devices = lax.axis_size("proto")
    images_all = img_local * batch_devices
    teacher_rows = WIDE_CROP_NUMBER * images_all
    student_count = crop_count * img_local
    unit_student, student_scale = unit_rows(student_features)
    student_bf = unit_student.astype(jnp.bfloat16).reshape(student_count, feature_dim)
    unit_proto, proto_scale = unit_columns(student_prototypes)
    proto_bf = unit_proto.astype(jnp.bfloat16)
    unit_teacher, unused_scale = unit_rows(teacher_features)
    teacher_bf = unit_teacher.astype(jnp.bfloat16).reshape(
        WIDE_CROP_NUMBER * img_local, feature_dim
    )
    unit_tproto, unused_tscale = unit_columns(teacher_prototypes)
    teacher_proto_bf = unit_tproto.astype(jnp.bfloat16)
    cluster_share = jnp.exp(
        jnp.dot(teacher_bf, teacher_proto_bf, preferred_element_type=jnp.float32) / TEACHER_TEMP
    )
    logits = jnp.dot(student_bf, proto_bf, preferred_element_type=jnp.float32) / STUDENT_TEMP
    exp_partial = jnp.sum(jnp.exp(logits), axis=1)
    for sweep_index in range(SK_ITERS):
        cluster_share = full_sweep(cluster_share, teacher_rows)
    exp_total = lax.psum(exp_partial, "proto")
    cluster_targets_matrix = (teacher_rows * cluster_share).reshape(
        WIDE_CROP_NUMBER, img_local, proto_local
    )
    first_global = cluster_targets_matrix[0]
    second_global = cluster_targets_matrix[1]
    summed = first_global + second_global
    targets = jnp.concatenate(
        [
            second_global[None],
            first_global[None],
            jnp.broadcast_to(summed[None], (crop_count - 2, img_local, proto_local)),
        ],
        axis=0,
    )
    pair_count = jnp.where(jnp.arange(crop_count) < 2, jnp.float32(1.0), jnp.float32(2.0))[
        :, None, None
    ]
    log_norm = jnp.log(exp_total).reshape(crop_count, img_local, 1)
    logits_crop = logits.reshape(crop_count, img_local, proto_local)
    loss_part = jnp.sum(targets * (log_norm - logits_crop))
    mean_loss = lax.psum(loss_part, ("batch", "proto")) / (images_all * PAIRS)
    factor = 1.0 / (images_all * PAIRS * STUDENT_TEMP)
    grad_cos = ((pair_count * jnp.exp(logits_crop - log_norm) - targets) * factor).astype(
        jnp.bfloat16
    )
    grad_cos = grad_cos.reshape(student_count, proto_local)
    feature_cot = lax.dot_general(
        grad_cos, proto_bf, (((1,), (1,)), ((), ())), preferred_element_type=jnp.float32
    )
    feature_cot = feature_cot.reshape(crop_count, img_local, feature_dim)
    own_count = img_local // proto_devices
    own_start = lax.axis_index("proto") * own_count
    cot_total = lax.psum(feature_cot, "proto")
    cot_own = lax.dynamic_slice_in_dim(cot_total, own_start, own_count, 1)
    unit_own = lax.dynamic_slice_in_dim(unit_student, own_start, own_count, 1)
    scale_own = lax.dynamic_slice_in_dim(student_scale, own_start, own_count, 1)
    grad_features = scale_own * (
        cot_own - unit_own * jnp.sum(unit_own * cot_own, axis=-1, keepdims=True)
    )
    curvature = jnp.sum(logits * STUDENT_TEMP * grad_cos.astype(jnp.float32), axis=0)
    rows_here = feature_dim // batch_devices
    product = lax.dot_general(
        student_bf, grad_cos, (((0,), (0,)), ((), ())), preferred_element_type=jnp.float32
    )
    term_total = lax.psum(product - unit_proto * curvature[None, :], "batch")
    term_own = lax.dynamic_slice_in_dim(
        term_total, lax.axis_index("batch") * rows_here, rows_here, 0
    )
    grad_prototypes = proto_scale * term_own
    return (mean_loss, grad_features, grad_prototypes)


def solution(mesh):
    placed = (P(None, "batch", None), P(None, "batch", None), P(None, "proto"), P(None, "proto"))
    return jax.shard_map(
        on_device,
        mesh=mesh,
        in_specs=placed,
        out_specs=(P(), P(None, ("batch", "proto"), None), P("batch", "proto")),
        check_vma=False,
    )
```

profile of v0, /device:TPU:1, one launch (start us, length us, event | category | flops | bytes accessed | tf_op | source)
XLA Modules:
  0.0 586.5 jit_solution(13375280952865046598)
XLA Ops:
  9.3 2.0 fusion.16
  11.3 4.6 fusion.46
  16.0 48.8 %psum.70 = f32[4096]{0:T(1024)S(1)} all-reduce(f32[4096]{0:T(1024)S(1)} %get-tuple-element.17), channel_id=1, replica_groups=mesh['batch'=16,'proto'=16] {'batch'}, use_global_device_ids=true, to_apply=%region_3.0 | all-reduce | flops 4096 | bytes 32768 | tf_op jit(solution)/shard_map/psum | solution.py:28
  64.8 2.6 divide_reduce_fusion
  67.3 33.6 %psum.71 = f32[256]{0:T(256)S(1)} all-reduce(f32[256]{0:T(256)S(1)} %divide_reduce_fusion), channel_id=1, replica_groups=mesh['batch'=16,'proto'=16] {'proto'}, use_global_device_ids=true, to_apply=%region_5.0 | all-reduce | flops 256 | bytes 2048 | tf_op jit(solution)/shard_map/psum | solution.py:34
  100.9 3.0 fusion.21
  103.9 52.8 %psum.72 = f32[4096]{0:T(1024)S(1)} all-reduce(f32[4096]{0:T(1024)S(1)} %fusion.21), channel_id=1, replica_groups=mesh['batch'=16,'proto'=16] {'batch'}, use_global_device_ids=true, to_apply=%region_7.0 | all-reduce | flops 4096 | bytes 32768 | tf_op jit(solution)/shard_map/psum | solution.py:28
  156.7 3.0 fusion.22
  159.7 28.5 %psum.73 = f32[256]{0:T(256)S(1)} all-reduce(f32[256]{0:T(256)S(1)} %fusion.22), channel_id=1, replica_groups=mesh['batch'=16,'proto'=16] {'proto'}, use_global_device_ids=true, to_apply=%region_9.0 | all-reduce | flops 256 | bytes 2048 | tf_op jit(solution)/shard_map/psum | solution.py:34
  188.2 3.2 fusion.23
  191.5 52.8 %psum.74 = f32[4096]{0:T(1024)S(1)} all-reduce(f32[4096]{0:T(1024)S(1)} %fusion.23), channel_id=1, replica_groups=mesh['batch'=16,'proto'=16] {'batch'}, use_global_device_ids=true, to_apply=%region_11.0 | all-reduce | flops 4096 | bytes 32768 | tf_op jit(solution)/shard_map/psum | solution.py:28
  244.3 3.4 fusion.24
  249.7 15.4 %broadcast_multiply_fusion = (f32[1280,4096]{1,0:T(8,128)}, f32[1280]{0:T(1024)S(1)}, f32[1280,4096]{1,0:T(8,128)}) fusion(bf16[1280,256]{1,0:T(8,128)(2,1)S(1)} %bitcast.37, bf16[256,4096]{1,0:T(8,128)(2,1)S(1)} %copy-done.1, f32[4096]{0:T(1024)S(1)} %add_rsqrt_fusion), kind=kOutput, calls=%fused_computation.10 | convolution fusion | flops 2697984768 | bytes 44717056 | tf_op jit(solution)/shard_map/dot_general | solution.py:59
  265.1 31.4 %all-reduce = (f32[256]{0:T(256)S(1)}, f32[1280]{0:T(1024)S(1)}) all-reduce(f32[256]{0:T(256)S(1)} %fusion.24, f32[1280]{0:T(1024)S(1)} %get-tuple-element.9), channel_id=1, replica_groups=mesh['batch'=16,'proto'=16] {'proto'}, use_global_device_ids=true, to_apply=%region_13.0 | all-reduce | flops 1536 | bytes 12288 | tf_op jit(solution)/shard_map/psum | solution.py:34
  296.5 3.5 fusion.20
  300.8 7.8 %broadcast_in_dim.8 = f32[8,128,4096]{2,1,0:T(8,128)} broadcast(f32[128,4096]{1,0:T(8,128)S(1)} %get-tuple-element.11), dimensions={1,2} | broadcast | bytes 18874368 | tf_op jit(solution)/shard_map/broadcast_in_dim | solution.py:74
  308.7 16.9 %pad_maximum_fusion = f32[10,128,4096]{2,1,0:T(8,128)} fusion(f32[8,128,4096]{2,1,0:T(8,128)} %broadcast_in_dim.8, f32[1,128,4096]{2,1,0:T(8,128)S(1)} %get-tuple-element.12, f32[1,128,4096]{2,1,0:T(8,128)S(1)} %get-tuple-element.10), kind=kLoop, calls=%fused_computation.1 | loop fusion | flops 10485760 | bytes 41943040 | tf_op jit(solution)/shard_map/concatenate | solution.py:70
  328.2 16.6 %multiply_reduce_fusion = (f32[4096]{0:T(1024)S(1)}, f32[]{:T(128)}, bf16[1280,4096]{1,0:T(8,128)(2,1)}) fusion(f32[1280,4096]{1,0:T(8,128)S(1)} %bitcast.34, f32[1280]{0:T(1024)S(1)} %get-tuple-element.16, f32[10,128,4096]{2,1,0:T(8,128)} %pad_maximum_fusion, f32[1280]{0:T(1024)S(1)} %broadcast_bitcast_fusion), kind=kLoop, calls=%fused_computation.7 | loop fusion | flops 62910464 | bytes 52455428 | tf_op jit(solution)/shard_map/reduce_sum | solution.py:103
  344.8 8.0 %fusion.26 = f32[10,128,256]{2,1,0:T(8,128)} fusion(bf16[10,128,4096]{2,1,0:T(8,128)(2,1)} %bitcast.36, bf16[256,4096]{1,0:T(8,128)(2,1)S(1)} %copy-done.2, f32[4096]{0:T(1024)S(1)} %add_rsqrt_fusion), kind=kOutput, calls=%fused_computation.40 | convolution fusion | flops 2687500288 | bytes 13910016 | tf_op jit(solution)/shard_map/dot_general | solution.py:90
  352.9 17.9 %fusion.13 = f32[256,4096]{1,0:T(8,128)} fusion(bf16[10,128,256]{2,1,0:T(8,128)(2,1)S(1)} %get-tuple-element.14, f32[10,128,4096]{2,1,0:T(8,128)} %bitcast.35, f32[10,128]{1,0:T(8,128)S(1)} %get-tuple-element.15, f32[10]{0:T(128)S(1)} %compare_select_fusion, bf16[256,4096]{1,0:T(8,128)(2,1)} %param.6, f32[8,128,4096]{2,1,0:T(8,128)} %broadcast_in_dim.8, ...), kind=kOutput, calls=%fused_computation.27 | convolution fusion | flops 2725249024 | bytes 48927784 | tf_op jit(solution)/shard_map/dot_general | solution.py:105
  370.8 82.0 %psum.77 = f32[]{:T(128)} all-reduce(f32[]{:T(128)} %get-tuple-element.4), channel_id=1, replica_groups=mesh['batch'=16,'proto'=16] {'batch','proto'}, use_global_device_ids=true, to_apply=%region_19.20 | all-reduce | flops 1 | bytes 8 | tf_op jit(solution)/shard_map/psum | solution.py:84
  453.5 1.8 fusion.35
  455.3 121.5 %all-reduce.6.cloned.1.call-done = f32[256,4096]{1,0:T(8,128)} async-done(((f32[256,4096]{1,0:T(8,128)}), f32[256,4096]{1,0:T(8,128)}) %all-reduce.6.cloned.1.call-update) | async-done | bytes 4194320 | tf_op jit(solution)/shard_map/psum | solution.py:108
  576.8 1.7 dynamic-slice_multiply_fusion
  (44 shorter events, 7.7 us)
Async XLA Ops:
  7.2 446.3 %all-reduce.4.cloned.1.call-start = ((), (), s32[]{:S(2)}) async-start(), calls=%async_computation | async-start | bytes 2621440 | tf_op jit(solution)/shard_map/psum | solution.py:96
  188.2 59.4 %copy-start.3 = (bf16[10,128,256]{2,1,0:T(8,128)(2,1)S(1)}, bf16[10,128,256]{2,1,0:T(8,128)(2,1)}, u32[]{:S(2)}) copy-start(bf16[10,128,256]{2,1,0:T(8,128)(2,1)} %param.4) | copy-start | bytes 1966084
  191.5 57.7 %copy-start.1 = (bf16[256,4096]{1,0:T(8,128)(2,1)S(1)}, bf16[256,4096]{1,0:T(8,128)(2,1)}, u32[]{:S(2)}) copy-start(bf16[256,4096]{1,0:T(8,128)(2,1)} %param.6) | copy-start | bytes 6291460
  300.7 7.9 %copy-start = (f32[1,128,4096]{2,1,0:T(8,128)}, f32[1,128,4096]{2,1,0:T(8,128)S(1)}, u32[]{:S(2)}) copy-start(f32[1,128,4096]{2,1,0:T(8,128)S(1)} %get-tuple-element.12) | copy-start | bytes 6291460
  308.6 17.0 %slice-start = ((s8[20971520]{0:T(1024)(128)(4,1)}), s8[4194304]{0:T(1024)(128)(4,1)S(1)}, s32[]{:S(2)}) async-start(s8[20971520]{0:T(1024)(128)(4,1)} %bitcast.33), calls=%async_computation.2 | async-start | bytes 8388608
  308.6 17.0 %slice-start.1 = ((s8[20971520]{0:T(1024)(128)(4,1)}), s8[4194304]{0:T(1024)(128)(4,1)S(1)}, s32[]{:S(2)}) async-start(s8[20971520]{0:T(1024)(128)(4,1)} %bitcast.33), calls=%async_computation.3 | async-start | bytes 8388608
  308.6 17.0 %slice-start.2 = ((s8[20971520]{0:T(1024)(128)(4,1)}), s8[4194304]{0:T(1024)(128)(4,1)S(1)}, s32[]{:S(2)}) async-start(s8[20971520]{0:T(1024)(128)(4,1)} %bitcast.33), calls=%async_computation.4 | async-start | bytes 8388608
  308.6 18.4 %slice-start.3 = ((s8[20971520]{0:T(1024)(128)(4,1)}), s8[4194304]{0:T(1024)(128)(4,1)S(1)}, s32[]{:S(2)}) async-start(s8[20971520]{0:T(1024)(128)(4,1)} %bitcast.33), calls=%async_computation.5 | async-start | bytes 8388608
  308.6 19.6 %slice-start.4 = ((s8[20971520]{0:T(1024)(128)(4,1)}), s8[4194304]{0:T(1024)(128)(4,1)S(1)}, s32[]{:S(2)}) async-start(s8[20971520]{0:T(1024)(128)(4,1)} %bitcast.33), calls=%async_computation.6 | async-start | bytes 8388608
  328.2 16.6 %copy-start.2 = (bf16[256,4096]{1,0:T(8,128)(2,1)S(1)}, bf16[256,4096]{1,0:T(8,128)(2,1)}, u32[]{:S(2)}) copy-start(bf16[256,4096]{1,0:T(8,128)(2,1)} %param.6) | copy-start | bytes 6291460
  352.8 224.0 %all-reduce.6.cloned.1.call-start = ((), (), s32[]{:S(2)}) async-start(), calls=%async_computation.1 | async-start | bytes 8388608 | tf_op jit(solution)/shard_map/psum | solution.py:108
Sparse Core Ops, SparseCore 0:
  352.9 99.8 all-reduce.3
  455.2 121.5 all-reduce.5
where the time goes:
time: 587 us; the launch traced here: 586 us
  blocking collectives  330 us (56%)
  waiting for transfers between devices  122 us (21%)
  other arithmetic  62.5 us (11%)
  matrix products  45.9 us (8%)
  between operations  16 us (3%)
  local copies, waits for them, and re-layouts  10.6 us (2%)
    psum x3, blocking collectives, proto_step(): column_mass = lax.psum(jnp.sum(cluster_share, axis=0), 'batch')  154 us
    psum x1, waiting for transfers between devices, on_device(): term_total = lax.psum(product - unit_proto * curvature[None, :], 'batch')  121 us
    psum x3, blocking collectives, full_sweep(): row_mass = lax.psum(jnp.sum(cluster_share, axis=1), 'proto')  93.5 us
    psum x1, blocking collectives, on_device(): mean_loss = lax.psum(loss_part, ('batch', 'proto')) / (images_all * PAIRS)  82 us
    dot_general x1, matrix products, on_device(): lax.dot_general(student_bf, grad_cos, (((0,), (0,)), ((), ())), preferred...  17.9 us
    concatenate x1, other arithmetic, on_device(): jnp.concatenate([second_global[None], first_global[None], jnp.broadcast_t...  16.9 us
    reduce_sum x1, other arithmetic, on_device(): jnp.sum(logits * STUDENT_TEMP * grad_cos.astype(jnp.float32), axis=0)  16.6 us
    dot_general x1, matrix products, on_device(): jnp.dot(student_bf, proto_bf, preferred_element_type=jnp.float32)  15.4 us
  transfers between devices with their start and end apart: 2, of which 1 were waited for; matrix products, arithmetic and copies ran while one was open for 3% of the time, Pallas kernels for 0%

commit v1 on v0

--- a/solution.py
+++ b/solution.py
@@ -10,6 +10,12 @@
 STUDENT_TEMP = 0.1
 TEACHER_TEMP = 0.07
 NORM_EPS = 1e-06
+
+
+def enter_area_on(xin):
+    back = jax.lax.all_gather(xin, axis_name="batch")
+    low = jnp.sum(back, axis=0)
+    return low
 
 
 def unit_rows(values):
@@ -25,7 +31,7 @@
 
 
 def proto_step(cluster_share):
-    column_mass = lax.psum(jnp.sum(cluster_share, axis=0), "batch")
+    column_mass = enter_area_on(jnp.sum(cluster_share, axis=0))
     return cluster_share / (CLUSTER_NUMBER * column_mass[None, :])
 
 

time: 587 us -> 498 us (0.85)
  blocking collectives: 330 us -> 240 us
    psum x3 -> x0, blocking collectives: 154 us -> none  [proto_step(): column_mass = lax.psum(jnp.sum(cluster_share, axis=0), 'batch')]
    all_gather x0 -> x3, blocking collectives: none -> 67.8 us  [enter_area_on(): back = jax.lax.all_gather(xin, axis_name='batch')]
  transfers between devices with their start and end apart: 2 -> 2, of which waited for: 1 -> 1; matrix products, arithmetic and copies ran while one was open for 3% -> 4% of each run, Pallas kernels for 0% -> 0%
where the time goes in v1:
time: 498 us; the launch traced here: 497 us
  blocking collectives  240 us (48%)
  waiting for transfers between devices  121 us (24%)
  other arithmetic  62.7 us (13%)
  matrix products  46.2 us (9%)
  between operations  16 us (3%)
  local copies, waits for them, and re-layouts  10.8 us (2%)
    psum x1, waiting for transfers between devices, on_device(): term_total = lax.psum(product - unit_proto * curvature[None, :], 'batch')  121 us
    psum x3, blocking collectives, full_sweep(): row_mass = lax.psum(jnp.sum(cluster_share, axis=1), 'proto')  93.3 us
    psum x1, blocking collectives, on_device(): mean_loss = lax.psum(loss_part, ('batch', 'proto')) / (images_all * PAIRS)  78.4 us
    all_gather x3, blocking collectives, enter_area_on(): back = jax.lax.all_gather(xin, axis_name='batch')  67.8 us
    dot_general x1, matrix products, on_device(): lax.dot_general(student_bf, grad_cos, (((0,), (0,)), ((), ())), preferred...  18.1 us
    concatenate x1, other arithmetic, on_device(): jnp.concatenate([second_global[None], first_global[None], jnp.broadcast_t...  16.9 us
    reduce_sum x1, other arithmetic, on_device(): jnp.sum(logits * STUDENT_TEMP * grad_cos.astype(jnp.float32), axis=0)  16.6 us
    dot_general x1, matrix products, on_device(): jnp.dot(student_bf, proto_bf, preferred_element_type=jnp.float32)  15.4 us
  transfers between devices with their start and end apart: 2, of which 1 were waited for; matrix products, arithmetic and copies ran while one was open for 4% of the time, Pallas kernels for 0%

profile of v1, /device:TPU:1, one launch (start us, length us, event | category | flops | bytes accessed | tf_op | source)
XLA Modules:
  0.0 496.9 jit_solution(8580483979239849079)
XLA Ops:
  9.3 2.0 fusion.16
  11.3 4.6 fusion.46
  16.0 22.0 %all-gather = f32[65536]{0:T(1024)S(1)} all-gather(f32[4096]{0:T(1024)S(1)} %get-tuple-element.17), channel_id=2, replica_groups=mesh['batch'=16,'proto'=16] {'batch'}, dimensions={0}, use_global_device_ids=true | all-gather | bytes 278528 | tf_op jit(solution)/shard_map/all_gather | solution.py:16
  38.1 2.6 divide_reduce_fusion
  40.6 33.5 %psum.49 = f32[256]{0:T(256)S(1)} all-reduce(f32[256]{0:T(256)S(1)} %divide_reduce_fusion), channel_id=1, replica_groups=mesh['batch'=16,'proto'=16] {'proto'}, use_global_device_ids=true, to_apply=%region_5.0 | all-reduce | flops 256 | bytes 2048 | tf_op jit(solution)/shard_map/psum | solution.py:40
  74.1 3.0 fusion.21
  77.1 22.1 %all-gather.1 = f32[65536]{0:T(1024)S(1)} all-gather(f32[4096]{0:T(1024)S(1)} %fusion.21), channel_id=3, replica_groups=mesh['batch'=16,'proto'=16] {'batch'}, dimensions={0}, use_global_device_ids=true | all-gather | bytes 278528 | tf_op jit(solution)/shard_map/all_gather | solution.py:16
  99.3 3.0 fusion.22
  102.3 28.5 %psum.50 = f32[256]{0:T(256)S(1)} all-reduce(f32[256]{0:T(256)S(1)} %fusion.22), channel_id=1, replica_groups=mesh['batch'=16,'proto'=16] {'proto'}, use_global_device_ids=true, to_apply=%region_9.0 | all-reduce | flops 256 | bytes 2048 | tf_op jit(solution)/shard_map/psum | solution.py:40
  130.8 3.2 fusion.23
  134.1 23.8 %all-gather.2 = f32[65536]{0:T(1024)S(1)} all-gather(f32[4096]{0:T(1024)S(1)} %fusion.23), channel_id=4, replica_groups=mesh['batch'=16,'proto'=16] {'batch'}, dimensions={0}, use_global_device_ids=true | all-gather | bytes 278528 | tf_op jit(solution)/shard_map/all_gather | solution.py:16
  157.9 3.5 fusion.24
  163.5 15.4 %broadcast_multiply_fusion = (f32[1280,4096]{1,0:T(8,128)}, f32[1280]{0:T(1024)S(1)}, f32[1280,4096]{1,0:T(8,128)}) fusion(bf16[1280,256]{1,0:T(8,128)(2,1)S(1)} %bitcast.37, bf16[256,4096]{1,0:T(8,128)(2,1)S(1)} %copy-done.1, f32[4096]{0:T(1024)S(1)} %add_rsqrt_fusion), kind=kOutput, calls=%fused_computation.10 | convolution fusion | flops 2697984768 | bytes 44717056 | tf_op jit(solution)/shard_map/dot_general | solution.py:65
  178.9 31.4 %all-reduce = (f32[256]{0:T(256)S(1)}, f32[1280]{0:T(1024)S(1)}) all-reduce(f32[256]{0:T(256)S(1)} %fusion.24, f32[1280]{0:T(1024)S(1)} %get-tuple-element.9), channel_id=1, replica_groups=mesh['batch'=16,'proto'=16] {'proto'}, use_global_device_ids=true, to_apply=%region_13.0 | all-reduce | flops 1536 | bytes 12288 | tf_op jit(solution)/shard_map/psum | solution.py:40
  210.3 3.5 fusion.20
  214.6 7.8 %broadcast_in_dim.8 = f32[8,128,4096]{2,1,0:T(8,128)} broadcast(f32[128,4096]{1,0:T(8,128)S(1)} %get-tuple-element.11), dimensions={1,2} | broadcast | bytes 18874368 | tf_op jit(solution)/shard_map/broadcast_in_dim | solution.py:80
  222.5 16.9 %pad_maximum_fusion = f32[10,128,4096]{2,1,0:T(8,128)} fusion(f32[8,128,4096]{2,1,0:T(8,128)} %broadcast_in_dim.8, f32[1,128,4096]{2,1,0:T(8,128)S(1)} %get-tuple-element.12, f32[1,128,4096]{2,1,0:T(8,128)S(1)} %get-tuple-element.10), kind=kLoop, calls=%fused_computation.1 | loop fusion | flops 10485760 | bytes 41943040 | tf_op jit(solution)/shard_map/concatenate | solution.py:76
  242.0 16.6 %multiply_reduce_fusion = (f32[4096]{0:T(1024)S(1)}, f32[]{:T(128)}, bf16[1280,4096]{1,0:T(8,128)(2,1)}) fusion(f32[1280,4096]{1,0:T(8,128)S(1)} %bitcast.34, f32[1280]{0:T(1024)S(1)} %get-tuple-element.16, f32[10,128,4096]{2,1,0:T(8,128)} %pad_maximum_fusion, f32[1280]{0:T(1024)S(1)} %broadcast_bitcast_fusion), kind=kLoop, calls=%fused_computation.7 | loop fusion | flops 62910464 | bytes 52455428 | tf_op jit(solution)/shard_map/reduce_sum | solution.py:109
  258.6 8.0 %fusion.26 = f32[10,128,256]{2,1,0:T(8,128)} fusion(bf16[10,128,4096]{2,1,0:T(8,128)(2,1)} %bitcast.36, bf16[256,4096]{1,0:T(8,128)(2,1)S(1)} %copy-done.2, f32[4096]{0:T(1024)S(1)} %add_rsqrt_fusion), kind=kOutput, calls=%fused_computation.40 | convolution fusion | flops 2687500288 | bytes 13910016 | tf_op jit(solution)/shard_map/dot_general | solution.py:96
  266.7 18.1 %fusion.13 = f32[256,4096]{1,0:T(8,128)} fusion(bf16[10,128,256]{2,1,0:T(8,128)(2,1)S(1)} %get-tuple-element.14, f32[10,128,4096]{2,1,0:T(8,128)} %bitcast.35, f32[10,128]{1,0:T(8,128)S(1)} %get-tuple-element.15, f32[10]{0:T(128)S(1)} %compare_select_fusion, bf16[256,4096]{1,0:T(8,128)(2,1)} %param.6, f32[8,128,4096]{2,1,0:T(8,128)} %broadcast_in_dim.8, ...), kind=kOutput, calls=%fused_computation.27 | convolution fusion | flops 2725249024 | bytes 48927784 | tf_op jit(solution)/shard_map/dot_general | solution.py:111
  284.9 78.4 %psum.53 = f32[]{:T(128)} all-reduce(f32[]{:T(128)} %get-tuple-element.4), channel_id=1, replica_groups=mesh['batch'=16,'proto'=16] {'batch','proto'}, use_global_device_ids=true, to_apply=%region_19.20 | all-reduce | flops 1 | bytes 8 | tf_op jit(solution)/shard_map/psum | solution.py:90
  364.0 1.8 fusion.35
  365.8 121.5 %all-reduce.6.cloned.1.call-done = f32[256,4096]{1,0:T(8,128)} async-done(((f32[256,4096]{1,0:T(8,128)}), f32[256,4096]{1,0:T(8,128)}) %all-reduce.6.cloned.1.call-update) | async-done | bytes 4194320 | tf_op jit(solution)/shard_map/psum | solution.py:114
  487.3 1.7 dynamic-slice_multiply_fusion
  (50 shorter events, 8.0 us)
Async XLA Ops:
  7.2 356.9 %all-reduce.4.cloned.1.call-start = ((), (), s32[]{:S(2)}) async-start(), calls=%async_computation | async-start | bytes 2621440 | tf_op jit(solution)/shard_map/psum | solution.py:102
  130.8 30.6 %copy-start.3 = (bf16[10,128,256]{2,1,0:T(8,128)(2,1)S(1)}, bf16[10,128,256]{2,1,0:T(8,128)(2,1)}, u32[]{:S(2)}) copy-start(bf16[10,128,256]{2,1,0:T(8,128)(2,1)} %param.4) | copy-start | bytes 1966084
  157.8 5.2 %copy-start.1 = (bf16[256,4096]{1,0:T(8,128)(2,1)S(1)}, bf16[256,4096]{1,0:T(8,128)(2,1)}, u32[]{:S(2)}) copy-start(bf16[256,4096]{1,0:T(8,128)(2,1)} %param.6) | copy-start | bytes 6291460
  214.5 7.9 %copy-start = (f32[1,128,4096]{2,1,0:T(8,128)}, f32[1,128,4096]{2,1,0:T(8,128)S(1)}, u32[]{:S(2)}) copy-start(f32[1,128,4096]{2,1,0:T(8,128)S(1)} %get-tuple-element.12) | copy-start | bytes 6291460
  222.4 17.0 %slice-start = ((s8[20971520]{0:T(1024)(128)(4,1)}), s8[4194304]{0:T(1024)(128)(4,1)S(1)}, s32[]{:S(2)}) async-start(s8[20971520]{0:T(1024)(128)(4,1)} %bitcast.33), calls=%async_computation.2 | async-start | bytes 8388608
  222.4 17.0 %slice-start.1 = ((s8[20971520]{0:T(1024)(128)(4,1)}), s8[4194304]{0:T(1024)(128)(4,1)S(1)}, s32[]{:S(2)}) async-start(s8[20971520]{0:T(1024)(128)(4,1)} %bitcast.33), calls=%async_computation.3 | async-start | bytes 8388608
  222.4 17.0 %slice-start.2 = ((s8[20971520]{0:T(1024)(128)(4,1)}), s8[4194304]{0:T(1024)(128)(4,1)S(1)}, s32[]{:S(2)}) async-start(s8[20971520]{0:T(1024)(128)(4,1)} %bitcast.33), calls=%async_computation.4 | async-start | bytes 8388608
  222.5 18.4 %slice-start.3 = ((s8[20971520]{0:T(1024)(128)(4,1)}), s8[4194304]{0:T(1024)(128)(4,1)S(1)}, s32[]{:S(2)}) async-start(s8[20971520]{0:T(1024)(128)(4,1)} %bitcast.33), calls=%async_computation.5 | async-start | bytes 8388608
  222.5 19.6 %slice-start.4 = ((s8[20971520]{0:T(1024)(128)(4,1)}), s8[4194304]{0:T(1024)(128)(4,1)S(1)}, s32[]{:S(2)}) async-start(s8[20971520]{0:T(1024)(128)(4,1)} %bitcast.33), calls=%async_computation.6 | async-start | bytes 8388608
  242.0 16.6 %copy-start.2 = (bf16[256,4096]{1,0:T(8,128)(2,1)S(1)}, bf16[256,4096]{1,0:T(8,128)(2,1)}, u32[]{:S(2)}) copy-start(bf16[256,4096]{1,0:T(8,128)(2,1)} %param.6) | copy-start | bytes 6291460
  266.6 220.7 %all-reduce.6.cloned.1.call-start = ((), (), s32[]{:S(2)}) async-start(), calls=%async_computation.1 | async-start | bytes 8388608 | tf_op jit(solution)/shard_map/psum | solution.py:114
Sparse Core Ops, SparseCore 0:
  266.8 96.5 all-reduce.3
  365.7 121.5 all-reduce.5
